TPU v7x, 32 devices: a whole 2x2x4 slice. The times are simulated.
32 devices in a mesh: seq: 8 (over y, x, core), mlp: 4 (over z).
Axes of the slice: x: 2, y: 2, z: 4, core: 2. Of those that a mesh axis runs over, the one named last changes fastest.
Arguments:
- query_rows: bfloat16 [2048, 8192], P('seq'), may hold values from -256 to 256
- key_rows: bfloat16 [2048, 1024], P(('seq', 'mlp')), may hold values from -6 to 6
- value_rows: bfloat16 [2048, 1024], P(('seq', 'mlp')), may hold values from -6 to 6
- key_blocks: int32 [64, 32, 16], P(None, 'seq'), may hold values from -1 to 31, as said below
Outputs:
- attention: bfloat16 [2048, 8192], P('seq', 'mlp')
Inputs may be any that keep to these rules, and one draw needn't show every extreme that they name: `key_blocks`: the list of head h and query block r names distinct blocks from 0 to r, always r itself, and holds -1 in its remaining slots; how many blocks a list names differs from head to head, and the longest list names exactly 16.
All inputs are finite; a program needn't handle non-finite values.
Results may differ from a plain program's by a relative error of at most 0.0075.
Values may be sent and summed in bfloat16 or wider, within the bound.
A program may use at most 128 MiB of HBM per device.

v0:
```python
import math

import jax
import jax.numpy as jnp
from jax import lax
from jax.sharding import PartitionSpec as P

H = 64
KVH = 8
HD = 128
BLK = 64


masked_score = -1e30


def choose_tile(length, rows_total):
    chosen = length
    for candidate in (128, 256, 512, 1024, 2048):
        if length % candidate == 0 and candidate * rows_total <= 4194304:
            chosen = candidate
    return chosen


def attend_tile(
    state, query_groups, key_tile, value_tile, key_pos, query_pos, listing, score_scale
):
    numerator, running_max, normalizer = state
    groups, rows_here, per_group, head_dim = query_groups.shape
    length = key_tile.shape[0]
    blocks_here = listing.shape[2]
    scores = (
        jnp.einsum("gtjd,ngd->gtjn", query_groups, key_tile, preferred_element_type=jnp.float32)
        * score_scale
    )
    key_block = key_pos // BLK
    named = jnp.any(listing[:, :, :, :, None] == key_block[None, None, None, None, :], axis=3)
    named = jnp.transpose(named, (0, 2, 1, 3))[:, :, None, :, :]
    named = jnp.broadcast_to(named, (groups, blocks_here, BLK, per_group, length)).reshape(
        groups, rows_here, per_group, length
    )
    allowed = named & (key_pos[None, None, None, :] <= query_pos[None, :, None, None])
    masked = jnp.where(allowed, scores, masked_score)
    new_max = jnp.maximum(running_max, jnp.max(masked, axis=3))
    probs = jnp.where(allowed, jnp.exp(masked - new_max[..., None]), 0.0)
    carried = jnp.exp(running_max - new_max)
    product = jnp.einsum(
        "gtjn,ngd->gtjd", probs.astype(jnp.bfloat16), value_tile, preferred_element_type=jnp.float32
    )
    numerator = numerator * carried[..., None] + product
    normalizer = normalizer * carried + jnp.sum(probs, axis=3)
    return (numerator, new_max, normalizer)


def fold_piece(state, pieces, key_pos, query_groups, listing, query_pos, score_scale):
    key_piece, value_piece = pieces
    length = key_piece.shape[0]
    groups, rows_here, per_group, head_dim = query_groups.shape
    tile = choose_tile(length, groups * rows_here * per_group)
    count = length // tile
    key_tiles = key_piece.reshape(count, tile, groups, head_dim)
    value_tiles = value_piece.reshape(count, tile, groups, head_dim)
    pos_tiles = key_pos.reshape(count, tile)

    def step(carry, tiles):
        return (
            attend_tile(
                carry, query_groups, tiles[0], tiles[1], tiles[2], query_pos, listing, score_scale
            ),
            None,
        )

    final, unused = lax.scan(step, state, (key_tiles, value_tiles, pos_tiles))
    return final


def empty_state(groups, rows_here, per_group, head_dim):
    return (
        jnp.zeros((groups, rows_here, per_group, head_dim), jnp.float32),
        jnp.full((groups, rows_here, per_group), masked_score, jnp.float32),
        jnp.zeros((groups, rows_here, per_group), jnp.float32),
    )


def body(query_rows, key_rows, value_rows, key_blocks):
    rows_here = query_rows.shape[0]
    per_group = H // KVH
    score_scale = 1.0 / math.sqrt(HD)
    query_pos = lax.axis_index("seq") * rows_here + jnp.arange(rows_here, dtype=jnp.int32)
    mlp_index = lax.axis_index("mlp")
    part_count = lax.axis_size("mlp")
    owned = KVH // part_count
    query_split = query_rows.reshape(rows_here, KVH, per_group, HD)
    listing_all = key_blocks.reshape(KVH, per_group, key_blocks.shape[1], key_blocks.shape[2])
    owned_keys, owned_values = (
        lax.all_to_all(key_rows, "mlp", split_axis=1, concat_axis=0, tiled=True),
        lax.all_to_all(value_rows, "mlp", split_axis=1, concat_axis=0, tiled=True),
    )
    query_own = lax.dynamic_slice_in_dim(query_split, mlp_index * owned, owned, 1)
    query_groups = jnp.transpose(query_own, (1, 0, 2, 3))
    listing_own = lax.dynamic_slice_in_dim(listing_all, mlp_index * owned, owned, 0)
    pieces = (
        lax.all_gather(owned_keys, "seq", axis=0, tiled=True),
        lax.all_gather(owned_values, "seq", axis=0, tiled=True),
    )
    length = pieces[0].shape[0]
    key_pos = jnp.arange(length, dtype=jnp.int32)
    numerator, running_max, normalizer = fold_piece(
        empty_state(owned, rows_here, per_group, HD),
        pieces,
        key_pos,
        query_groups,
        listing_own,
        query_pos,
        score_scale,
    )
    result = (numerator / normalizer[..., None]).astype(jnp.bfloat16)
    return jnp.transpose(result, (1, 0, 2, 3)).reshape(rows_here, owned * per_group * HD)


def solution(mesh):
    placed = (
        P("seq", None),
        P(("seq", "mlp"), None),
        P(("seq", "mlp"), None),
        P(None, "seq", None),
    )
    return jax.shard_map(
        body, mesh=mesh, in_specs=placed, out_specs=P("seq", "mlp"), check_vma=False
    )
```

profile of v0, /device:TPU:5, one launch (start us, length us, event | category | flops | bytes accessed | tf_op | source)
XLA Modules:
  0.0 146.3 jit_solution(11475522339148334712)
XLA Ops:
  6.5 0.9 copy.66
  7.5 9.3 %all_to_all.38 = bf16[64,4,256]{2,0,1:T(8,128)(2,1)} all-to-all(bf16[64,4,256]{2,0,1:T(8,128)(2,1)S(1)} %bitcast.82), channel_id=1, replica_groups=mesh['seq'=8,'mlp'=4] {'mlp'}, dimensions={1} | all-to-all | bytes 262144 | tf_op jit(solution)/shard_map/all_to_all | solution.py:96
  16.8 0.9 copy.65
  17.8 8.1 %all_to_all.39 = bf16[64,4,256]{2,0,1:T(8,128)(2,1)} all-to-all(bf16[64,4,256]{2,0,1:T(8,128)(2,1)S(1)} %bitcast.83), channel_id=1, replica_groups=mesh['seq'=8,'mlp'=4] {'mlp'}, dimensions={1} | all-to-all | bytes 262144 | tf_op jit(solution)/shard_map/all_to_all | solution.py:97
  25.9 0.9 copy.39
  26.8 6.4 %copy.41 = bf16[256,8192]{0,1:T(8,128)(2,1)} copy(bf16[256,8192]{1,0:T(8,128)(2,1)} %param.6) | data formatting | bytes 8388608 | tf_op args[0]
  33.2 1.3 dynamic-slice_bitcast_fusion
  34.5 0.7 copy.44
  35.2 6.2 %all-gather.3.cloned.1.call-done = bf16[2048,256]{1,0:T(8,128)(2,1)} async-done(((bf16[256,256]{1,0:T(8,128)(2,1)}), bf16[2048,256]{1,0:T(8,128)(2,1)}) %all-gather.3.cloned.1.call-update) | async-done | bytes 1048592 | tf_op jit(solution)/shard_map/all_gather | solution.py:103
  41.4 2.1 %reshape.117 = bf16[2,1024,2,128]{3,2,1,0:T(2,128)(2,1)} reshape(bf16[2048,256]{1,0:T(8,128)(2,1)} %all-gather.3.cloned.1.call-done) | data formatting | bytes 2097152 | tf_op jit(solution)/shard_map/reshape | solution.py:61
  43.5 23.3 %all-gather.5.cloned.1.call-done = bf16[2048,256]{1,0:T(8,128)(2,1)} async-done(((bf16[256,256]{1,0:T(8,128)(2,1)}), bf16[2048,256]{1,0:T(8,128)(2,1)}) %all-gather.5.cloned.1.call-update) | async-done | bytes 1048592 | tf_op jit(solution)/shard_map/all_gather | solution.py:104
  66.8 2.2 %reshape.119 = bf16[2,1024,2,128]{3,2,1,0:T(2,128)(2,1)} reshape(bf16[2048,256]{1,0:T(8,128)(2,1)} %all-gather.5.cloned.1.call-done) | data formatting | bytes 2097152 | tf_op jit(solution)/shard_map/reshape | solution.py:62
  69.0 66.6 %while.17 = (s32[]{:T(128)}, f32[2,256,8,128]{3,1,2,0:T(8,128)}, f32[2,256,8]{1,2,0:T(8,128)S(1)}, f32[2,256,8]{1,2,0:T(8,128)S(1)}, s32[2,8,4,16]{3,2,1,0:T(4,1...) while((s32[]{:T(128)}, f32[2,256,8,128]{3,1,2,0:T(8,128)}, ...), condition=%wide.region_4.5_spmd.clone, body=%wide.region_0.4_spmd.clone.sunk | while | flops 2218495232 | bytes 102267048 | solution.py:73
  69.0 1.0 compare_reduce_fusion.2
  70.0 0.2 broadcast_compare_fusion.2
  70.2 1.9 %constant_dynamic-slice_fusion.7 = (bf16[1,1024,2,128]{3,2,1,0:T(2,128)(2,1)S(1)}, bf16[1,1024,2,128]{3,2,1,0:T(2,128)(2,1)S(1)}) fusion(bf16[2,1024,2,128]{3,2,1,0:T(2,128)(2,1)} %get-tuple-element.341, s32[]{:T(128)S(6)} %copy.79, bf16[2,1024,2,128]{3,2,1,0:T(2,128)(2,1)} %get-tuple-element.339), kind=kLoop, calls=%fused_computation.27.clone.1 | loop fusion | bytes 2097156 | tf_op jit(solution)/shard_map/while/body/jit(dynamic_index_in_dim)/dynamic_slice | solution.py:73
  72.1 1.3 broadcast_in_dim.66
  73.4 9.4 %copy.74 = pred[2,256,8,1024]{1,3,2,0:T(32,128)(4,1)S(1)} copy(pred[2,256,8,1024]{3,2,1,0:T(8,128)(4,1)S(1)} %bitcast.74) | data formatting | bytes 8388608 | tf_op jit(solution)/shard_map/while/body/eval_jaxpr/reshape | solution.py:39
  82.8 4.0 %fusion.28 = (f32[2,256,8]{1,2,0:T(8,128)S(1)}, f32[2,1024,256,8]{2,1,3,0:T(8,128)S(1)}) fusion(pred[2,256,8,1024]{1,3,2,0:T(32,128)(4,1)S(1)} %copy.74, pred[256,1024]{0,1:T(8,128)(4,1)S(1)} %broadcast_compare_fusion.2, bf16[2,256,8,128]{3,1,2,0:T(8,128)(2,1)S(1)} %get-tuple-element.340, bf16[1,1024,2,128]{3,2,1,0:T(2,128)(2,1)S(1)} %get-tuple-element.303), kind=kOutput, calls=%fused_computation.3.clone.1 | convolution fusion | flops 1090514944 | bytes 22822912 | tf_op jit(solution)/shard_map/while/body/eval_jaxpr/gtjd,ngd->gtjn/dot_general | solution.py:33
  86.9 5.6 %fusion.29 = f32[2,256,8]{1,2,0:T(8,128)S(1)} fusion(f32[2,1024,256,8]{2,1,3,0:T(8,128)S(1)} %get-tuple-element.304, pred[2,256,8,1024]{1,3,2,0:T(32,128)(4,1)S(1)} %copy.74, f32[2,256,8]{1,2,0:T(8,128)S(1)} %select_maximum_fusion.2, pred[256,1024]{0,1:T(8,128)(4,1)S(1)} %broadcast_compare_fusion.2), kind=kLoop, calls=%fused_computation.4.clone.1 | loop fusion | flops 25161728 | bytes 21266432 | tf_op jit(solution)/shard_map/while/body/eval_jaxpr/reduce_sum | solution.py:51
  92.5 9.6 %fusion.31 = f32[2,256,8,128]{3,1,2,0:T(8,128)} fusion(f32[2,256,8,128]{3,1,2,0:T(8,128)} %get-tuple-element.322, f32[2,1024,256,8]{2,1,3,0:T(8,128)S(1)} %get-tuple-element.304, pred[2,256,8,1024]{1,3,2,0:T(32,128)(4,1)} %copy-done, f32[2,256,8]{1,2,0:T(8,128)S(1)} %select_maximum_fusion.2, pred[256,1024]{0,1:T(8,128)(4,1)S(1)} %broadcast_compare_fusion.2, ...), kind=kOutput, calls=%fused_computation.10.clone.1 | convolution fusion | flops 1100480512 | bytes 25985024 | tf_op jit(solution)/shard_map/while/body/eval_jaxpr/gtjn,ngd->gtjd/dot_general | solution.py:47
  102.2 1.0 compare_reduce_fusion.2
  103.2 0.2 broadcast_compare_fusion.2
  103.4 1.9 %constant_dynamic-slice_fusion.7 = (bf16[1,1024,2,128]{3,2,1,0:T(2,128)(2,1)S(1)}, bf16[1,1024,2,128]{3,2,1,0:T(2,128)(2,1)S(1)}) fusion(bf16[2,1024,2,128]{3,2,1,0:T(2,128)(2,1)} %get-tuple-element.341, s32[]{:T(128)S(6)} %copy.79, bf16[2,1024,2,128]{3,2,1,0:T(2,128)(2,1)} %get-tuple-element.339), kind=kLoop, calls=%fused_computation.27.clone.1 | loop fusion | bytes 2097156 | tf_op jit(solution)/shard_map/while/body/jit(dynamic_index_in_dim)/dynamic_slice | solution.py:73
  105.3 1.3 broadcast_in_dim.66
  106.6 9.4 %copy.74 = pred[2,256,8,1024]{1,3,2,0:T(32,128)(4,1)S(1)} copy(pred[2,256,8,1024]{3,2,1,0:T(8,128)(4,1)S(1)} %bitcast.74) | data formatting | bytes 8388608 | tf_op jit(solution)/shard_map/while/body/eval_jaxpr/reshape | solution.py:39
  116.0 4.0 %fusion.28 = (f32[2,256,8]{1,2,0:T(8,128)S(1)}, f32[2,1024,256,8]{2,1,3,0:T(8,128)S(1)}) fusion(pred[2,256,8,1024]{1,3,2,0:T(32,128)(4,1)S(1)} %copy.74, pred[256,1024]{0,1:T(8,128)(4,1)S(1)} %broadcast_compare_fusion.2, bf16[2,256,8,128]{3,1,2,0:T(8,128)(2,1)S(1)} %get-tuple-element.340, bf16[1,1024,2,128]{3,2,1,0:T(2,128)(2,1)S(1)} %get-tuple-element.303), kind=kOutput, calls=%fused_computation.3.clone.1 | convolution fusion | flops 1090514944 | bytes 22822912 | tf_op jit(solution)/shard_map/while/body/eval_jaxpr/gtjd,ngd->gtjn/dot_general | solution.py:33
  120.1 5.6 %fusion.29 = f32[2,256,8]{1,2,0:T(8,128)S(1)} fusion(f32[2,1024,256,8]{2,1,3,0:T(8,128)S(1)} %get-tuple-element.304, pred[2,256,8,1024]{1,3,2,0:T(32,128)(4,1)S(1)} %copy.74, f32[2,256,8]{1,2,0:T(8,128)S(1)} %select_maximum_fusion.2, pred[256,1024]{0,1:T(8,128)(4,1)S(1)} %broadcast_compare_fusion.2), kind=kLoop, calls=%fused_computation.4.clone.1 | loop fusion | flops 25161728 | bytes 21266432 | tf_op jit(solution)/shard_map/while/body/eval_jaxpr/reduce_sum | solution.py:51
  125.7 9.9 %fusion.31 = f32[2,256,8,128]{3,1,2,0:T(8,128)} fusion(f32[2,256,8,128]{3,1,2,0:T(8,128)} %get-tuple-element.322, f32[2,1024,256,8]{2,1,3,0:T(8,128)S(1)} %get-tuple-element.304, pred[2,256,8,1024]{1,3,2,0:T(32,128)(4,1)} %copy-done, f32[2,256,8]{1,2,0:T(8,128)S(1)} %select_maximum_fusion.2, pred[256,1024]{0,1:T(8,128)(4,1)S(1)} %broadcast_compare_fusion.2, ...), kind=kOutput, calls=%fused_computation.10.clone.1 | convolution fusion | flops 1100480512 | bytes 25985024 | tf_op jit(solution)/shard_map/while/body/eval_jaxpr/gtjn,ngd->gtjd/dot_general | solution.py:47
  135.6 1.9 %fusion.18 = bf16[256,2,8,128]{3,0,2,1:T(8,128)(2,1)S(1)} fusion(f32[2,256,8,128]{3,1,2,0:T(8,128)} %get-tuple-element.132, f32[2,256,8]{1,2,0:T(8,128)S(1)} %get-tuple-element.133), kind=kLoop, calls=%fused_computation.36 | loop fusion | flops 1048576 | bytes 3162112 | tf_op jit(solution)/shard_map/transpose | solution.py:118
  137.5 0.7 copy.46
  138.2 1.2 copy.64
  (27 shorter events, 0.3 us)
Async XLA Ops:
  6.5 34.9 %all-gather.3.cloned.1.call-start = ((), (), s32[]{:S(2)}) async-start(), calls=%async_computation.2 | async-start | bytes 1179648 | tf_op jit(solution)/shard_map/all_gather | solution.py:103
  16.8 50.0 %all-gather.5.cloned.1.call-start = ((), (), s32[]{:S(2)}) async-start(), calls=%async_computation.3 | async-start | bytes 1179648 | tf_op jit(solution)/shard_map/all_gather | solution.py:104
  82.8 4.1 %copy-start = (pred[2,256,8,1024]{1,3,2,0:T(32,128)(4,1)}, pred[2,256,8,1024]{1,3,2,0:T(32,128)(4,1)S(1)}, u32[]{:S(2)}) copy-start(pred[2,256,8,1024]{1,3,2,0:T(32,128)(4,1)S(1)} %copy.74) | copy-start | bytes 12582916 | tf_op jit(solution)/shard_map/while
  116.0 4.1 %copy-start = (pred[2,256,8,1024]{1,3,2,0:T(32,128)(4,1)}, pred[2,256,8,1024]{1,3,2,0:T(32,128)(4,1)S(1)}, u32[]{:S(2)}) copy-start(pred[2,256,8,1024]{1,3,2,0:T(32,128)(4,1)S(1)} %copy.74) | copy-start | bytes 12582916 | tf_op jit(solution)/shard_map/while
Sparse Core Ops, SparseCore 0:
  16.9 24.4 all-gather.2
  43.3 23.4 all-gather.4
where the time goes:
time: 148 us; the launch traced here: 146 us
  local copies, waits for them, and re-layouts  42.5 us (29%)
  waiting for transfers between devices  29.5 us (20%)
  matrix products  27.6 us (19%)
  blocking collectives  17.4 us (12%)
  other arithmetic  15.5 us (10%)
  between operations  13.5 us (9%)
    all_gather x1, waiting for transfers between devices, body(): lax.all_gather(owned_values, 'seq', axis=0, tiled=True)  23.3 us
    dot_general x2, matrix products, attend_tile(): jnp.einsum('gtjn,ngd->gtjd', probs.astype(jnp.bfloat16), value_tile, pref...  19.5 us
    reshape x2, local copies, waits for them, and re-layouts, attend_tile(): jnp.broadcast_to(named, (groups, blocks_here, BLK, per_group, length))  18.8 us
    reduce_sum x2, other arithmetic, attend_tile(): normalizer = normalizer * carried + jnp.sum(probs, axis=3)  11.2 us
    all_to_all x1, blocking collectives, body(): lax.all_to_all(key_rows, 'mlp', split_axis=1, concat_axis=0, tiled=True)  9.31 us
    unnamed x4, local copies, waits for them, and re-layouts  9.18 us
    dot_general x2, matrix products, attend_tile(): jnp.einsum('gtjd,ngd->gtjn', query_groups, key_tile, preferred_element_ty...  8.09 us
    all_to_all x1, blocking collectives, body(): lax.all_to_all(value_rows, 'mlp', split_axis=1, concat_axis=0, tiled=True)  8.09 us
  transfers between devices with their start and end apart: 2, of which 2 were waited for; matrix products, arithmetic and copies ran while one was open for 8% of the time, Pallas kernels for 0%

commit v1 on v0

v1 whole, which is shorter than its diff:
```python
import functools
import math

import jax
import jax.numpy as jnp
from jax import lax
from jax.experimental import pallas as pl
from jax.experimental.pallas import tpu as pltpu
from jax.sharding import PartitionSpec as P

H = 64
KVH = 8
HD = 128
BLK = 64
PER_GROUP = H // KVH

MESH = pl.DeviceIdType.MESH
MASKED = -1e30
FAR = 1e9


def kernel(
    n_seq, n_mlp, list_s, list_v, q_hbm, k_hbm, v_hbm, out_ref,
    kbuf, vbuf, qbuf, kpos, probs, norm,
    local_sem, z_send, z_recv, hop_send, hop_recv, relay_send, own_sib_send, sib_send, sib_recv,
):
    s = lax.axis_index("seq")
    m = lax.axis_index("mlp")
    chips = n_seq // 2
    p, c = s // 2, s % 2
    piece = k_hbm.shape[0]
    rows = piece * n_mlp
    width = kbuf.shape[2]
    heads = H // n_mlp
    kmax = list_s.shape[2]
    q_blocks = rows // BLK
    srcs = (k_hbm, v_hbm)
    bufs = (kbuf, vbuf)
    sibling = 2 * p + 1 - c

    def piece_rows(src_s, z):
        return src_s * n_mlp + z

    def columns(z):
        return pl.ds(pl.multiple_of(z * width, width), width)

    def z_copy(a, to):
        return pltpu.make_async_remote_copy(
            src_ref=srcs[a].at[:, columns(to)], dst_ref=bufs[a].at[piece_rows(s, m)],
            send_sem=z_send.at[a, to], recv_sem=z_recv.at[a, m],
            device_id=(s, to), device_id_type=MESH)

    def z_arrival(a, z):
        return pltpu.make_async_remote_copy(
            src_ref=srcs[a].at[:, columns(z)], dst_ref=bufs[a].at[piece_rows(s, z)],
            send_sem=z_send.at[a, z], recv_sem=z_recv.at[a, z],
            device_id=(s, z), device_id_type=MESH)

    def moved(a, src_p, src_c, z, to_s, send, recv):
        part = bufs[a].at[piece_rows(2 * src_p + src_c, z)]
        return pltpu.make_async_remote_copy(
            src_ref=part, dst_ref=part, send_sem=send, recv_sem=recv,
            device_id=(to_s, m), device_id_type=MESH)

    def own_copy(a, z, to_p):
        return moved(a, p, c, z, 2 * to_p + c, hop_send.at[a, z, to_p], hop_recv.at[a, z, p])

    def hop_arrival(a, z, src_p):
        return moved(a, src_p, c, z, 2 * src_p + c, hop_send.at[a, z, src_p], hop_recv.at[a, z, src_p])

    def relay_copy(a, z, src_p, to_p):
        return moved(a, src_p, c, z, 2 * to_p + c, relay_send.at[a, z], hop_recv.at[a, z, src_p])

    def own_sib_copy(a, z):
        return moved(a, p, c, z, sibling, own_sib_send.at[a, z], sib_recv.at[a, z, p])

    def sib_copy(a, z, src_p):
        return moved(a, src_p, c, z, sibling, sib_send.at[a, z, src_p], sib_recv.at[a, z, src_p])

    def sib_arrival(a, z, src_p):
        return moved(a, src_p, 1 - c, z, sibling, sib_send.at[a, z, src_p], sib_recv.at[a, z, src_p])

    def relays(src_p):
        if chips != 4:
            return []
        zero = jnp.logical_and(src_p == 0, jnp.logical_or(
            jnp.logical_and(p == 1, c == 0), jnp.logical_and(p == 2, c == 1)))
        one = jnp.logical_and(src_p == 1, p == 3)
        return [(zero, 3), (one, 2)]

    def direct(to_p):
        if chips != 4:
            return to_p >= 0
        return jnp.logical_not(jnp.logical_or(
            jnp.logical_and(p == 0, to_p == 3), jnp.logical_and(p == 1, to_p == 2)))

    def send_own(a, z):
        @pl.loop(p + 1, chips)
        def _(to_p):
            @pl.when(direct(to_p))
            def _():
                own_copy(a, z, to_p).start()

        @pl.when(c == 0)
        def _():
            own_sib_copy(a, z).start()

    def pass_on(a, z, src_p):
        hop_arrival(a, z, src_p).wait_recv()
        for wanted, to_p in relays(src_p):
            @pl.when(wanted)
            def _():
                relay_copy(a, z, src_p, to_p).start()
        sib_copy(a, z, src_p).start()

    def z_order(i):
        return lax.rem(m + i, n_mlp)

    def local_copy(a):
        return pltpu.make_async_copy(
            srcs[a].at[:, columns(m)], bufs[a].at[piece_rows(s, m)], local_sem.at[a])

    q_copy = pltpu.make_async_copy(
        q_hbm.at[:, pl.ds(pl.multiple_of(m * heads * HD, heads * HD), heads * HD)], qbuf, local_sem.at[2])
    local_copy(0).start()
    local_copy(1).start()
    q_copy.start()

    barrier = pltpu.get_barrier_semaphore()

    @pl.loop(1, n_mlp)
    def _(i):
        pl.semaphore_signal(barrier, inc=1, device_id=(s, z_order(i)), device_id_type=MESH)

    @pl.loop(1, chips)
    def _(i):
        pl.semaphore_signal(
            barrier, inc=1, device_id=(2 * lax.rem(p + i, chips) + c, m), device_id_type=MESH)

    pl.semaphore_signal(barrier, inc=1, device_id=(sibling, m), device_id_type=MESH)
    pl.semaphore_wait(barrier, n_mlp - 1 + chips - 1 + 1)

    for a in range(2):
        @pl.loop(1, n_mlp)
        def _(i):
            z_copy(a, z_order(i)).start()

    for a in range(2):
        local_copy(a).wait()
        send_own(a, m)
        if a == 0:
            spread = (lax.broadcasted_iota(jnp.int32, (kmax, kmax * BLK), 1) // BLK
                      == lax.broadcasted_iota(jnp.int32, (kmax, kmax * BLK), 0)).astype(jnp.bfloat16)
            inside = (lax.broadcasted_iota(jnp.int32, (q_blocks, kmax * BLK), 1) % BLK).astype(jnp.float32)

            @pl.loop(0, heads)
            def _(h):
                named = list_v[m * heads + h].astype(jnp.float32).astype(jnp.bfloat16)
                block = jnp.dot(named, spread, preferred_element_type=jnp.float32)
                kpos[h] = jnp.where(block < 0, FAR, block * BLK + inside)

        @pl.loop(1, n_mlp)
        def _(i):
            z = z_order(i)
            z_arrival(a, z).wait_recv()
            send_own(a, z)

    @pl.loop(0, p * n_mlp)
    def _(i):
        pass_on(0, lax.rem(i, n_mlp), i // n_mlp)

    def finish(a):
        @pl.loop(0, (p + c) * n_mlp)
        def _(i):
            sib_arrival(a, lax.rem(i, n_mlp), i // n_mlp).wait_recv()

    finish(0)
    q_copy.wait()

    factor = math.log2(math.e) / math.sqrt(HD)
    first = s * rows
    per_head = -(-(chips - 1) * n_mlp // heads)

    def lanes(index, size):
        return pl.ds(pl.multiple_of(index * size, size), size)

    def gathered(buf, h, qb):
        group = lanes(h // PER_GROUP, HD)
        parts = []
        for k in range(kmax):
            block = jnp.maximum(list_s[m * heads + h, qb, k], 0)
            parts.append(buf[block, :, group])
        return jnp.concatenate(parts, axis=0)

    @pl.loop(0, heads)
    def _(h):
        for j in range(per_head):
            i = h * per_head + j

            @pl.when(i < p * n_mlp)
            def _():
                pass_on(1, lax.rem(i, n_mlp), i // n_mlp)

        positions = kpos[h]
        for qb in range(q_blocks):
            queries = qbuf[qb * BLK:(qb + 1) * BLK, lanes(h, HD)]
            scores = lax.dot_general(
                queries, gathered(kbuf, h, qb), (((1,), (1,)), ((), ())),
                preferred_element_type=jnp.float32)
            row = (lax.broadcasted_iota(jnp.int32, (BLK, 1), 0) + (first + qb * BLK)).astype(jnp.float32)
            scores = jnp.where(positions[qb:qb + 1, :] <= row, scores, MASKED)
            top = jnp.max(scores, axis=1, keepdims=True)
            weights = jnp.exp2((scores - top) * factor)
            total = jnp.sum(weights, axis=1, keepdims=True)
            probs[h, qb * BLK:(qb + 1) * BLK, :] = weights.astype(jnp.bfloat16)
            norm[h, qb * BLK:(qb + 1) * BLK, :] = jnp.broadcast_to(total, (BLK, HD))

    finish(1)

    @pl.loop(0, heads)
    def _(h):
        for qb in range(q_blocks):
            part = slice(qb * BLK, (qb + 1) * BLK)
            product = jnp.dot(probs[h, part, :], gathered(vbuf, h, qb), preferred_element_type=jnp.float32)
            out_ref[part, lanes(h, HD)] = (product / norm[h, part, :]).astype(out_ref.dtype)

    for a in range(2):
        @pl.loop(1, n_mlp)
        def _(i):
            z_copy(a, z_order(i)).wait_send()

        @pl.loop(0, n_mlp)
        def _(z):
            @pl.loop(p + 1, chips)
            def _(to_p):
                @pl.when(direct(to_p))
                def _():
                    own_copy(a, z, to_p).wait_send()

            @pl.when(c == 0)
            def _():
                own_sib_copy(a, z).wait_send()

            @pl.loop(0, p)
            def _(src_p):
                for wanted, to_p in relays(src_p):
                    @pl.when(wanted)
                    def _():
                        relay_copy(a, z, src_p, to_p).wait_send()
                sib_copy(a, z, src_p).wait_send()


def body(n_seq, n_mlp, query_rows, key_rows, value_rows, key_blocks):
    piece = key_rows.shape[0]
    rows = query_rows.shape[0]
    tokens = rows * n_seq
    heads = H // n_mlp
    width = (KVH // n_mlp) * HD
    kmax = key_blocks.shape[2]
    chips = n_seq // 2
    dma = pltpu.SemaphoreType.DMA
    return pl.pallas_call(
        functools.partial(kernel, n_seq, n_mlp),
        out_shape=jax.ShapeDtypeStruct((rows, heads * HD), jnp.bfloat16),
        in_specs=[
            pl.BlockSpec(memory_space=pltpu.SMEM),
            pl.BlockSpec(memory_space=pltpu.VMEM),
            pl.BlockSpec(memory_space=pl.ANY),
            pl.BlockSpec(memory_space=pl.ANY),
            pl.BlockSpec(memory_space=pl.ANY),
        ],
        out_specs=pl.BlockSpec(memory_space=pltpu.VMEM),
        scratch_shapes=[
            pltpu.VMEM((tokens // BLK, BLK, width), jnp.bfloat16),
            pltpu.VMEM((tokens // BLK, BLK, width), jnp.bfloat16),
            pltpu.VMEM((rows, heads * HD), jnp.bfloat16),
            pltpu.VMEM((heads, rows // BLK, kmax * BLK), jnp.float32),
            pltpu.VMEM((heads, rows, kmax * BLK), jnp.bfloat16),
            pltpu.VMEM((heads, rows, HD), jnp.float32),
            dma((3,)),
            dma((2, n_mlp)),
            dma((2, n_mlp)),
            dma((2, n_mlp, chips)),
            dma((2, n_mlp, chips)),
            dma((2, n_mlp)),
            dma((2, n_mlp)),
            dma((2, n_mlp, chips)),
            dma((2, n_mlp, chips)),
        ],
        compiler_params=pltpu.CompilerParams(
            collective_id=0, has_side_effects=True, vmem_limit_bytes=58 * 1024 * 1024),
        name="block_sparse_attention",
    )(key_blocks, key_blocks, query_rows, key_rows, value_rows)


def solution(mesh):
    placed = (
        P("seq", None),
        P(("seq", "mlp"), None),
        P(("seq", "mlp"), None),
        P(None, "seq", None),
    )
    return jax.shard_map(
        functools.partial(body, mesh.shape["seq"], mesh.shape["mlp"]),
        mesh=mesh, in_specs=placed, out_specs=P("seq", "mlp"), check_vma=False
    )
```

time: 148 us -> 52.1 us (0.35)
  Pallas kernels: 0 us -> 47.2 us
  local copies, waits for them, and re-layouts: 42.5 us -> 3.82 us
  waiting for transfers between devices: 29.5 us -> 0 us
  matrix products: 27.6 us -> 0 us
  blocking collectives: 17.4 us -> 0 us
  other arithmetic: 15.5 us -> 0 us
  between operations: 13.5 us -> 0.01 us
    pallas_call x0 -> x1, Pallas kernels: none -> 47.2 us  [body(): pl.pallas_call(functools.partial(kernel, n_seq, n_mlp), out_shape=jax.Sha...]
    all_gather x2 -> x0, waiting for transfers between devices: 29.5 us -> none  [the longest x1 23.3 us: body(): lax.all_gather(owned_values, 'seq', axis=0, tiled=True)]
    dot_general x4 -> x0, matrix products: 27.6 us -> none  [the longest x2 19.5 us: attend_tile(): jnp.einsum('gtjn,ngd->gtjd', probs.astype(jnp.bfloat16), value_tile, pref...]
    reshape x4 -> x0, local copies, waits for them, and re-layouts: 23.1 us -> none  [the longest x2 18.8 us: attend_tile(): jnp.broadcast_to(named, (groups, blocks_here, BLK, per_group, length))]
    all_to_all x2 -> x0, blocking collectives: 17.4 us -> none  [the longest x1 9.31 us: body(): lax.all_to_all(key_rows, 'mlp', split_axis=1, concat_axis=0, tiled=True)]
    reduce_sum x2 -> x0, other arithmetic: 11.2 us -> none  [attend_tile(): normalizer = normalizer * carried + jnp.sum(probs, axis=3)]
    unnamed x4 -> x2, local copies, waits for them, and re-layouts: 9.18 us -> 3.82 us
    dynamic_slice x5 -> x0, local copies, waits for them, and re-layouts: 3.89 us -> none  [the longest x4 3.87 us: fold_piece(): final, unused = lax.scan(step, state, (key_tiles, value_tiles, pos_tiles))]
  transfers between devices with their start and end apart: 2 -> 0, of which waited for: 2 -> 0; matrix products, arithmetic and copies ran while one was open for 8% -> 0% of each run, Pallas kernels for 0% -> 0%
where the time goes in v1:
time: 52.1 us; the launch traced here: 51.1 us
  Pallas kernels  47.2 us (91%)
  local copies, waits for them, and re-layouts  3.82 us (7%)
    pallas_call x1, Pallas kernels, body(): pl.pallas_call(functools.partial(kernel, n_seq, n_mlp), out_shape=jax.Sha...  47.2 us
    unnamed x2, local copies, waits for them, and re-layouts  3.82 us

profile of v1, /device:TPU:5, one launch (start us, length us, event | category | flops | bytes accessed | tf_op | source)
XLA Modules:
  0.0 51.1 jit_solution(6463851807897787549)
XLA Ops:
  0.0 1.5 %copy.5.list_s.list_v = s32[64,4,16]{2,1,0:T(4,128)} copy(s32[64,4,16]{0,2,1:T(8,128)} %param.7) | data formatting | bytes 32768 | tf_op args[3]
  1.5 47.2 %block_sparse_attention.1 = bf16[256,2048]{1,0:T(8,128)(2,1)} custom-call(s32[64,4,16]{2,1,0:T(4,128)} %copy.5.list_s.list_v, s32[64,4,16]{2,1,0:T(4,128)} %copy.5.list_s.list_v, bf16[256,8192]{1,0:T(8,128)(2,1)} %q_hbm.1, bf16[64,1024]{1,0:T(8,128)(2,1)} %k_hbm.1, bf16[64,1024]{1,0:T(8,128)(2,1)} %v_hbm.1), custom_call_target="tpu_custom_call" | custom-call | tf_op jit(solution)/shard_map/block_sparse_attention/pallas_call | solution.py:262
  48.7 2.3 %copy.8 = bf16[256,2048]{1,0:T(8,128)(2,1)} copy(bf16[256,2048]{1,0:T(8,128)(2,1)} %block_sparse_attention.1) | data formatting | bytes 2097152

commit v2 on v0

v2 whole, which is shorter than its diff:
```python
import functools
import math

import jax
import jax.numpy as jnp
from jax import lax
from jax.experimental import pallas as pl
from jax.experimental.pallas import tpu as pltpu
from jax.sharding import PartitionSpec as P

H = 64
KVH = 8
HD = 128
BLK = 64
PER_GROUP = H // KVH

MESH = pl.DeviceIdType.MESH
MASKED = -1e30
FAR = 1e9


def gather_kernel(
    n_seq, n_mlp, list_v, k_hbm, v_hbm, kv, kpos, own_list, used,
    local_sem, z_send, z_recv, hop_send, hop_recv, own_sib_send, sib_send, sib_recv,
):
    s = lax.axis_index("seq")
    m = lax.axis_index("mlp")
    chips = n_seq // 2
    p, c = s // 2, s % 2
    width = kv.shape[3]
    heads, q_blocks, kmax = own_list.shape
    srcs = (k_hbm, v_hbm)
    sibling = 2 * p + 1 - c

    def columns(z):
        return pl.ds(pl.multiple_of(z * width, width), width)

    def z_copy(a, to):
        return pltpu.make_async_remote_copy(
            src_ref=srcs[a].at[:, columns(to)], dst_ref=kv.at[s * n_mlp + m, a],
            send_sem=z_send.at[a, to], recv_sem=z_recv.at[a, m],
            device_id=(s, to), device_id_type=MESH)

    def z_arrival(a, z):
        return pltpu.make_async_remote_copy(
            src_ref=srcs[a].at[:, columns(z)], dst_ref=kv.at[s * n_mlp + z, a],
            send_sem=z_send.at[a, z], recv_sem=z_recv.at[a, z],
            device_id=(s, z), device_id_type=MESH)

    def moved(src_p, src_c, z, to_s, send, recv):
        part = kv.at[(2 * src_p + src_c) * n_mlp + z]
        return pltpu.make_async_remote_copy(
            src_ref=part, dst_ref=part, send_sem=send, recv_sem=recv,
            device_id=(to_s, m), device_id_type=MESH)

    def own_copy(z, to_p):
        return moved(p, c, z, 2 * to_p + c, hop_send.at[z, to_p], hop_recv.at[z, p])

    def hop_arrival(z, src_p):
        return moved(src_p, c, z, 2 * src_p + c, hop_send.at[z, src_p], hop_recv.at[z, src_p])

    def own_sib_copy(z):
        return moved(p, c, z, sibling, own_sib_send.at[z], sib_recv.at[z, p])

    def sib_copy(z, src_p):
        return moved(src_p, c, z, sibling, sib_send.at[z, src_p], sib_recv.at[z, src_p])

    def sib_arrival(z, src_p):
        return moved(src_p, 1 - c, z, sibling, sib_send.at[z, src_p], sib_recv.at[z, src_p])

    def send_own(z):
        @pl.loop(p + 1, chips)
        def _(to_p):
            own_copy(z, to_p).start()

        @pl.when(c == 0)
        def _():
            own_sib_copy(z).start()

    def z_order(i):
        return lax.rem(m + i, n_mlp)

    def local_copy(a):
        return pltpu.make_async_copy(
            srcs[a].at[:, columns(m)], kv.at[s * n_mlp + m, a], local_sem.at[a])

    local_copy(0).start()
    local_copy(1).start()

    barrier = pltpu.get_barrier_semaphore()

    @pl.loop(1, n_mlp)
    def _(i):
        pl.semaphore_signal(barrier, inc=1, device_id=(s, z_order(i)), device_id_type=MESH)

    @pl.loop(1, chips)
    def _(i):
        pl.semaphore_signal(
            barrier, inc=1, device_id=(2 * lax.rem(p + i, chips) + c, m), device_id_type=MESH)

    pl.semaphore_signal(barrier, inc=1, device_id=(sibling, m), device_id_type=MESH)
    pl.semaphore_wait(barrier, n_mlp - 1 + chips - 1 + 1)

    @pl.loop(1, n_mlp)
    def _(i):
        z_copy(0, z_order(i)).start()
        z_copy(1, z_order(i)).start()

    local_copy(0).wait()
    local_copy(1).wait()
    send_own(m)

    listing = list_v[pl.ds(m * heads, heads)]
    own_list[...] = jnp.maximum(listing, 0)
    slots = lax.broadcasted_iota(jnp.int32, listing.shape, 2) + 1
    most = jnp.max(jnp.where(listing >= 0, slots, 0), axis=2, keepdims=True)
    used[...] = jnp.broadcast_to(jnp.max(most, axis=1, keepdims=True), used.shape)
    spread = (lax.broadcasted_iota(jnp.int32, (kmax, kmax * BLK), 1) // BLK
              == lax.broadcasted_iota(jnp.int32, (kmax, kmax * BLK), 0)).astype(jnp.bfloat16)
    inside = (lax.broadcasted_iota(jnp.int32, (q_blocks, kmax * BLK), 1) % BLK).astype(jnp.float32)

    @pl.loop(0, heads)
    def _(h):
        named = list_v[m * heads + h].astype(jnp.float32).astype(jnp.bfloat16)
        block = jnp.dot(named, spread, preferred_element_type=jnp.float32)
        kpos[h] = jnp.where(block < 0, FAR, block * BLK + inside)

    @pl.loop(1, n_mlp)
    def _(i):
        z = z_order(i)
        z_arrival(0, z).wait_recv()
        z_arrival(1, z).wait_recv()
        send_own(z)

    @pl.loop(0, n_mlp)
    def _(i):
        @pl.loop(0, p)
        def _(src_p):
            z = z_order(i)
            hop_arrival(z, src_p).wait_recv()
            sib_copy(z, src_p).start()

    @pl.loop(0, n_mlp)
    def _(z):
        @pl.loop(0, p + c)
        def _(src_p):
            sib_arrival(z, src_p).wait_recv()

    @pl.loop(1, n_mlp)
    def _(i):
        z_copy(0, z_order(i)).wait_send()
        z_copy(1, z_order(i)).wait_send()

    @pl.loop(0, n_mlp)
    def _(z):
        @pl.loop(p + 1, chips)
        def _(to_p):
            own_copy(z, to_p).wait_send()

        @pl.when(c == 0)
        def _():
            own_sib_copy(z).wait_send()

        @pl.loop(0, p)
        def _(src_p):
            sib_copy(z, src_p).wait_send()


def attend_kernel(
    own_list, used, kpos, q_hbm, kv_hbm, out_hbm, kbuf, vbuf, qbuf, out_buf, sem, out_sem,
):
    s = lax.axis_index("seq")
    m = lax.axis_index("mlp")
    heads, q_blocks, kmax = own_list.shape
    rows = q_blocks * BLK
    wide = heads * HD

    k_copy = pltpu.make_async_copy(kv_hbm.at[:, 0], kbuf, sem.at[0])
    v_copy = pltpu.make_async_copy(kv_hbm.at[:, 1], vbuf, sem.at[1])
    q_copy = pltpu.make_async_copy(
        q_hbm.at[:, pl.ds(pl.multiple_of(m * wide, wide), wide)], qbuf, sem.at[2])
    k_copy.start()
    q_copy.start()
    v_copy.start()

    factor = math.log2(math.e) / math.sqrt(HD)
    first = s * rows

    def lanes(index):
        return pl.ds(pl.multiple_of(index * HD, HD), HD)

    def out_copy(h):
        return pltpu.make_async_copy(out_buf.at[:, lanes(h)], out_hbm.at[:, lanes(h)], out_sem.at[h])

    def gathered(buf, h, qb, count):
        group = lanes(h // PER_GROUP)
        return jnp.concatenate([buf[own_list[h, qb, k], :, group] for k in range(count)], axis=0)

    def one_head(h, count):
        parts = [slice(qb * BLK, (qb + 1) * BLK) for qb in range(q_blocks)]
        scores = [
            lax.dot_general(
                qbuf[parts[qb], lanes(h)], gathered(kbuf, h, qb, count), (((1,), (1,)), ((), ())),
                preferred_element_type=jnp.float32)
            for qb in range(q_blocks)]
        positions = kpos[h, :, :count * BLK]
        weights, totals = [], []
        for qb in range(q_blocks):
            row = (lax.broadcasted_iota(jnp.int32, (BLK, 1), 0) + (first + qb * BLK)).astype(jnp.float32)
            masked = jnp.where(positions[qb:qb + 1, :] <= row, scores[qb], MASKED)
            top = jnp.max(masked, axis=1, keepdims=True)
            raised = jnp.exp2((masked - top) * factor)
            totals.append(jnp.sum(raised, axis=1, keepdims=True))
            weights.append(raised.astype(jnp.bfloat16))
        for qb in range(q_blocks):
            product = jnp.dot(weights[qb], gathered(vbuf, h, qb, count), preferred_element_type=jnp.float32)
            out_buf[parts[qb], lanes(h)] = (product / totals[qb]).astype(out_buf.dtype)

    k_copy.wait()
    q_copy.wait()
    v_copy.wait()
    steps = [kmax * i // 4 for i in range(1, 5)]

    @pl.loop(0, heads)
    def _(h):
        need = used[h, 0, 0]
        for low, high in zip([0] + steps, steps):
            @pl.when(jnp.logical_and(need > low, need <= high))
            def _():
                one_head(h, high)

        out_copy(h).start()

    @pl.loop(0, heads)
    def _(h):
        out_copy(h).wait()


def body(n_seq, n_mlp, query_rows, key_rows, value_rows, key_blocks):
    piece = key_rows.shape[0]
    rows = query_rows.shape[0]
    heads = H // n_mlp
    width = (KVH // n_mlp) * HD
    q_blocks, kmax = key_blocks.shape[1:]
    chips = n_seq // 2
    blocks = n_seq * n_mlp
    dma = pltpu.SemaphoreType.DMA
    whole = pl.BlockSpec(memory_space=pltpu.VMEM)
    anywhere = pl.BlockSpec(memory_space=pl.ANY)
    scalars = pl.BlockSpec(memory_space=pltpu.SMEM)
    kv, kpos, own_list, used = pl.pallas_call(
        functools.partial(gather_kernel, n_seq, n_mlp),
        out_shape=(
            jax.ShapeDtypeStruct((blocks, 2, piece, width), jnp.bfloat16),
            jax.ShapeDtypeStruct((heads, q_blocks, kmax * BLK), jnp.float32),
            jax.ShapeDtypeStruct((heads, q_blocks, kmax), jnp.int32),
            jax.ShapeDtypeStruct((heads, 1, 128), jnp.int32),
        ),
        in_specs=[whole, anywhere, anywhere],
        out_specs=(anywhere, whole, whole, whole),
        scratch_shapes=[
            dma((2,)),
            dma((2, n_mlp)),
            dma((2, n_mlp)),
            dma((n_mlp, chips)),
            dma((n_mlp, chips)),
            dma((n_mlp,)),
            dma((n_mlp, chips)),
            dma((n_mlp, chips)),
        ],
        compiler_params=pltpu.CompilerParams(collective_id=0, has_side_effects=True),
        name="gather_keys_values",
    )(key_blocks, key_rows, value_rows)
    return pl.pallas_call(
        attend_kernel,
        out_shape=jax.ShapeDtypeStruct((rows, heads * HD), jnp.bfloat16),
        in_specs=[scalars, scalars, whole, anywhere, anywhere],
        out_specs=anywhere,
        scratch_shapes=[
            pltpu.VMEM((blocks, piece, width), jnp.bfloat16),
            pltpu.VMEM((blocks, piece, width), jnp.bfloat16),
            pltpu.VMEM((rows, heads * HD), jnp.bfloat16),
            pltpu.VMEM((rows, heads * HD), jnp.bfloat16),
            dma((3,)),
            dma((heads,)),
        ],
        compiler_params=pltpu.CompilerParams(vmem_limit_bytes=48 * 1024 * 1024),
        name="attend_listed_blocks",
    )(own_list, used, kpos, query_rows, kv)


def solution(mesh):
    placed = (
        P("seq", None),
        P(("seq", "mlp"), None),
        P(("seq", "mlp"), None),
        P(None, "seq", None),
    )
    return jax.shard_map(
        functools.partial(body, mesh.shape["seq"], mesh.shape["mlp"]),
        mesh=mesh, in_specs=placed, out_specs=P("seq", "mlp"), check_vma=False
    )
```

time: 148 us -> 43.2 us (0.29)
  the two profiles are of different devices: /device:TPU:5 before, /device:TPU:15 now
where the time goes in v2:
time: 43.2 us; the launch traced here: 42.4 us
  Pallas kernels  36.9 us (85%)
  local copies, waits for them, and re-layouts  5.5 us (13%)
    pallas_call x1, Pallas kernels, body(): pl.pallas_call(functools.partial(gather_kernel, n_seq, n_mlp), out_shape=...  23.5 us
    pallas_call x1, Pallas kernels, body(): pl.pallas_call(attend_kernel, out_shape=jax.ShapeDtypeStruct((rows, heads...  13.4 us
    unnamed x9, local copies, waits for them, and re-layouts  5.5 us

profile of v2, /device:TPU:15, one launch (start us, length us, event | category | flops | bytes accessed | tf_op | source)
XLA Modules:
  0.0 42.4 jit_solution(16779261656444688827)
XLA Ops:
  0.0 1.5 %copy.5.list_v = s32[64,4,16]{2,1,0:T(4,128)} copy(s32[64,4,16]{0,2,1:T(8,128)} %param.7) | data formatting | bytes 32768 | tf_op args[3]
  1.5 23.5 %gather_keys_values.1 = (bf16[32,2,64,256]{3,2,1,0:T(8,128)(2,1)}, f32[16,4,1024]{2,1,0:T(4,128)}, s32[16,4,16]{2,1,0:T(4,128)}, s32[16,1,128]{2,1,0:T(1,128)}) custom-call(s32[64,4,16]{2,1,0:T(4,128)} %copy.5.list_v, bf16[64,1024]{1,0:T(8,128)(2,1)} %k_hbm.1, bf16[64,1024]{1,0:T(8,128)(2,1)} %v_hbm.1), custom_call_target="tpu_custom_call" | custom-call | tf_op jit(solution)/shard_map/gather_keys_values/pallas_call | solution.py:251
  25.0 0.0 copy-start
  25.0 1.6 %copy-done = bf16[32,2,64,256]{3,2,1,0:T(8,128)(2,1)S(1)} copy-done((bf16[32,2,64,256]{3,2,1,0:T(8,128)(2,1)S(1)}, bf16[32,2,64,256]{3,2,1,0:T(8,128)(2,1)}, u32[]{:S(2)}) %copy-start) | copy-done | bytes 2097176
  26.6 0.0 copy-start.1
  26.6 0.9 %copy-done.1 = f32[16,4,1024]{2,1,0:T(4,128)S(1)} copy-done((f32[16,4,1024]{2,1,0:T(4,128)S(1)}, f32[16,4,1024]{2,1,0:T(4,128)}, u32[]{:S(2)}) %copy-start.1) | copy-done | bytes 262168
  27.5 0.0 copy-start.2
  27.5 0.8 %copy-done.2 = s32[16,4,16]{2,1,0:T(4,128)S(1)} copy-done((s32[16,4,16]{2,1,0:T(4,128)S(1)}, s32[16,4,16]{2,1,0:T(4,128)}, u32[]{:S(2)}) %copy-start.2) | copy-done | bytes 4120
  28.3 0.0 copy-start.3
  28.3 0.7 %copy-done.3 = s32[16,1,128]{2,1,0:T(1,128)S(1)} copy-done((s32[16,1,128]{2,1,0:T(1,128)S(1)}, s32[16,1,128]{2,1,0:T(1,128)}, u32[]{:S(2)}) %copy-start.3) | copy-done | bytes 8216
  29.0 13.4 %attend_listed_blocks.1 = bf16[256,2048]{1,0:T(8,128)(2,1)} custom-call(s32[16,4,16]{2,1,0:T(4,128)S(1)} %copy-done.2, s32[16,1,128]{2,1,0:T(1,128)S(1)} %copy-done.3, f32[16,4,1024]{2,1,0:T(4,128)S(1)} %copy-done.1, bf16[256,8192]{1,0:T(8,128)(2,1)} %q_hbm.1, bf16[32,2,64,256]{3,2,1,0:T(8,128)(2,1)S(1)} %copy-done), custom_call_target="tpu_custom_call" | custom-call | tf_op jit(solution)/shard_map/attend_listed_blocks/pallas_call | solution.py:274
Async XLA Ops:
  25.0 1.6 %copy-start = (bf16[32,2,64,256]{3,2,1,0:T(8,128)(2,1)S(1)}, bf16[32,2,64,256]{3,2,1,0:T(8,128)(2,1)}, u32[]{:S(2)}) copy-start(bf16[32,2,64,256]{3,2,1,0:T(8,128)(2,1)} %get-tuple-element.12.kv_hbm) | copy-start | bytes 6291460
  26.6 0.9 %copy-start.1 = (f32[16,4,1024]{2,1,0:T(4,128)S(1)}, f32[16,4,1024]{2,1,0:T(4,128)}, u32[]{:S(2)}) copy-start(f32[16,4,1024]{2,1,0:T(4,128)} %get-tuple-element.11.kpos) | copy-start | bytes 786436
  27.5 0.8 %copy-start.2 = (s32[16,4,16]{2,1,0:T(4,128)S(1)}, s32[16,4,16]{2,1,0:T(4,128)}, u32[]{:S(2)}) copy-start(s32[16,4,16]{2,1,0:T(4,128)} %get-tuple-element.9.own_list) | copy-start | bytes 12292
  28.3 0.7 %copy-start.3 = (s32[16,1,128]{2,1,0:T(1,128)S(1)}, s32[16,1,128]{2,1,0:T(1,128)}, u32[]{:S(2)}) copy-start(s32[16,1,128]{2,1,0:T(1,128)} %get-tuple-element.10.used) | copy-start | bytes 24580

commit v3 on v1

v3 whole, which is shorter than its diff:
```python
import functools
import math

import jax
import jax.numpy as jnp
from jax import lax
from jax.experimental import pallas as pl
from jax.experimental.pallas import tpu as pltpu
from jax.sharding import PartitionSpec as P

H = 64
KVH = 8
HD = 128
BLK = 64
PER_GROUP = H // KVH

MESH = pl.DeviceIdType.MESH
MASKED = -1e30
FAR = 1e9


def lanes(index, size=HD):
    return pl.ds(pl.multiple_of(index * size, size), size)


def score_kernel(
    n_seq, n_mlp, list_s, list_v, q_hbm, k_hbm, v_hbm, v_out, p_out, plan,
    kbuf, qbuf, kpos, spaced, probs,
    local_sem, p_sem, z_send, z_recv, hop_send, hop_recv, own_sib_send, sib_send, sib_recv,
):
    s = lax.axis_index("seq")
    m = lax.axis_index("mlp")
    chips = n_seq // 2
    p, c = s // 2, s % 2
    width = kbuf.shape[2]
    q_blocks, kmax = list_v.shape[:2]
    heads = H // n_mlp
    together = 4 if kmax <= 16 else 1
    srcs = (k_hbm, v_hbm)
    bufs = (kbuf, v_out)
    sibling = 2 * p + 1 - c

    def z_copy(a, to):
        return pltpu.make_async_remote_copy(
            src_ref=srcs[a].at[:, lanes(to, width)], dst_ref=bufs[a].at[s * n_mlp + m],
            send_sem=z_send.at[a, to], recv_sem=z_recv.at[a, m],
            device_id=(s, to), device_id_type=MESH)

    def z_arrival(a, z):
        return pltpu.make_async_remote_copy(
            src_ref=srcs[a].at[:, lanes(z, width)], dst_ref=bufs[a].at[s * n_mlp + z],
            send_sem=z_send.at[a, z], recv_sem=z_recv.at[a, z],
            device_id=(s, z), device_id_type=MESH)

    def moved(a, src_p, src_c, z, to_s, send, recv):
        part = bufs[a].at[(2 * src_p + src_c) * n_mlp + z]
        return pltpu.make_async_remote_copy(
            src_ref=part, dst_ref=part, send_sem=send, recv_sem=recv,
            device_id=(to_s, m), device_id_type=MESH)

    def own_copy(a, z, to_p):
        return moved(a, p, c, z, 2 * to_p + c, hop_send.at[a, z, to_p], hop_recv.at[a, z, p])

    def hop_arrival(a, z, src_p):
        return moved(a, src_p, c, z, 2 * src_p + c, hop_send.at[a, z, src_p], hop_recv.at[a, z, src_p])

    def own_sib_copy(a, z):
        return moved(a, p, c, z, sibling, own_sib_send.at[a, z], sib_recv.at[a, z, p])

    def sib_copy(a, z, src_p):
        return moved(a, src_p, c, z, sibling, sib_send.at[a, z, src_p], sib_recv.at[a, z, src_p])

    def sib_arrival(a, z, src_p):
        return moved(a, src_p, 1 - c, z, sibling, sib_send.at[a, z, src_p], sib_recv.at[a, z, src_p])

    def send_own(a, z):
        @pl.loop(p + 1, chips)
        def _(to_p):
            own_copy(a, z, to_p).start()

        @pl.when(c == 0)
        def _():
            own_sib_copy(a, z).start()

    def pass_on(a, z):
        @pl.loop(0, p)
        def _(src_p):
            hop_arrival(a, z, src_p).wait_recv()
            sib_copy(a, z, src_p).start()

    def finish(a):
        @pl.loop(0, n_mlp)
        def _(z):
            @pl.loop(0, p + c)
            def _(src_p):
                sib_arrival(a, z, src_p).wait_recv()

    def z_order(i):
        if n_mlp != 4:
            return lax.rem(m + i, n_mlp)
        second = jnp.where(jnp.logical_or(m == 0, m == 2), 1, 2)
        third = jnp.where(m == 0, 2, jnp.where(m == 1, 0, jnp.where(m == 2, 3, 1)))
        last = jnp.where(m < 2, 3, 0)
        return jnp.where(i == 0, m, jnp.where(i == 1, second, jnp.where(i == 2, third, last)))

    def local_copy(a):
        return pltpu.make_async_copy(
            srcs[a].at[:, lanes(m, width)], bufs[a].at[s * n_mlp + m], local_sem.at[a])

    q_copy = pltpu.make_async_copy(q_hbm.at[:, lanes(m, heads * HD)], qbuf, local_sem.at[2])
    local_copy(0).start()
    local_copy(1).start()

    barrier = pltpu.get_barrier_semaphore()

    @pl.loop(1, n_mlp)
    def _(i):
        pl.semaphore_signal(barrier, inc=1, device_id=(s, z_order(i)), device_id_type=MESH)

    @pl.loop(1, chips)
    def _(i):
        pl.semaphore_signal(
            barrier, inc=1, device_id=(2 * lax.rem(p + i, chips) + c, m), device_id_type=MESH)

    pl.semaphore_signal(barrier, inc=1, device_id=(sibling, m), device_id_type=MESH)
    pl.semaphore_wait(barrier, n_mlp - 1 + chips - 1 + 1)

    for a in range(2):
        @pl.loop(1, n_mlp)
        def _(i):
            z_copy(a, z_order(i)).start()

    q_copy.start()
    for a in range(2):
        local_copy(a).wait()
        send_own(a, m)

        @pl.loop(1, n_mlp)
        def _(i):
            z = z_order(i)
            z_arrival(a, z).wait_recv()
            send_own(a, z)

    slots = lax.broadcasted_iota(jnp.int32, list_v.shape, 1) + 1
    most = jnp.max(jnp.where(list_v[...] >= 0, slots, 0), axis=1)
    used = jnp.max(most, axis=0, keepdims=True).astype(jnp.float32)
    across = lax.broadcasted_iota(jnp.int32, (H, H), 1)
    down = lax.broadcasted_iota(jnp.int32, (H, H), 0)
    other = jnp.broadcast_to(used, (H, H))
    mine = jnp.sum(jnp.where(across == down, other, 0.0), axis=1, keepdims=True)
    ahead = jnp.logical_or(other > mine, jnp.logical_and(other == mine, across < down))
    ahead = jnp.logical_and(ahead, across // heads == down // heads)
    rank = jnp.sum(jnp.where(ahead, 1.0, 0.0), axis=1, keepdims=True)
    holds = jnp.logical_and(rank == across.astype(jnp.float32), down // heads == m)
    order = jnp.sum(jnp.where(holds, (down - m * heads).astype(jnp.float32), 0.0), axis=0, keepdims=True)
    plan_row = lax.broadcasted_iota(jnp.int32, plan.shape, 0)
    plan[...] = jnp.where(plan_row == 0, used, order).astype(jnp.int32)

    spread = (lax.broadcasted_iota(jnp.int32, (kmax, kmax * BLK), 1) // BLK
              == lax.broadcasted_iota(jnp.int32, (kmax, kmax * BLK), 0)).astype(jnp.bfloat16)
    inside = (lax.broadcasted_iota(jnp.int32, (heads, kmax * BLK), 1) % BLK).astype(jnp.float32)
    for qb in range(q_blocks):
        named = list_v[qb].astype(jnp.float32).astype(jnp.bfloat16)
        spaced[...] = lax.dot_general(
            named, spread, (((0,), (0,)), ((), ())), preferred_element_type=jnp.float32)
        block = spaced[pl.ds(pl.multiple_of(m * heads, heads), heads), :]
        kpos[qb] = jnp.where(block < 0, FAR, block * BLK + inside)

    @pl.loop(0, n_mlp)
    def _(i):
        pass_on(0, z_order(i))

    finish(0)
    q_copy.wait()

    factor = math.log2(math.e) / math.sqrt(HD)
    first = s * q_blocks * BLK
    parts = [slice(qb * BLK, (qb + 1) * BLK) for qb in range(q_blocks)]
    row_in_block = lax.broadcasted_iota(jnp.int32, (BLK, 1), 0)
    steps = heads // together

    def p_copy(t):
        some = pl.ds(t * together, together)
        return pltpu.make_async_copy(probs.at[some], p_out.at[some], p_sem.at[t])

    @pl.loop(0, steps)
    def _(t):
        scores = {}

        def score(h, j):
            for qb in range(q_blocks):
                names = [jnp.maximum(list_s[qb, k, m * heads + h], 0) for k in range(kmax)]
                keys = jnp.concatenate([kbuf[b, :, lanes(h // PER_GROUP)] for b in names], axis=0)
                scores[j, qb] = lax.dot_general(
                    qbuf[parts[qb], lanes(h)], keys, (((1,), (1,)), ((), ())),
                    preferred_element_type=jnp.float32)

        def weigh(h, j):
            for qb in range(q_blocks):
                row = (row_in_block + (first + qb * BLK)).astype(jnp.float32)
                masked = jnp.where(kpos[qb, pl.ds(h, 1), :] <= row, scores.pop((j, qb)), MASKED)
                top = jnp.max(masked, axis=1, keepdims=True)
                raised = jnp.exp2((masked - top) * factor)
                scale = 1.0 / jnp.sum(raised, axis=1, keepdims=True)
                probs[h, parts[qb], :] = (raised * scale).astype(probs.dtype)

        for j in range(together + 1):
            if j > 0:
                weigh(t * together + j - 1, j - 1)
            if j < together:
                score(t * together + j, j)
        p_copy(t).start()
        if steps == n_mlp:
            pass_on(1, z_order(t))

    if steps != n_mlp:
        @pl.loop(0, n_mlp)
        def _(i):
            pass_on(1, z_order(i))

    finish(1)

    @pl.loop(0, steps)
    def _(t):
        p_copy(t).wait()

    for a in range(2):
        @pl.loop(1, n_mlp)
        def _(i):
            z_copy(a, z_order(i)).wait_send()

        @pl.loop(0, n_mlp)
        def _(z):
            @pl.loop(p + 1, chips)
            def _(to_p):
                own_copy(a, z, to_p).wait_send()

            @pl.when(c == 0)
            def _():
                own_sib_copy(a, z).wait_send()

            @pl.loop(0, p)
            def _(src_p):
                sib_copy(a, z, src_p).wait_send()


def combine_kernel(
    list_hbm, plan_hbm, p_hbm, v_hbm, out_hbm, listing, plan, pbuf, vbuf, out_buf, sem, p_sem, out_sem,
):
    m = lax.axis_index("mlp")
    q_blocks, kmax = listing.shape[:2]
    heads = pbuf.shape[0]
    together = 4 if kmax <= 16 else 1
    parts = [slice(qb * BLK, (qb + 1) * BLK) for qb in range(q_blocks)]

    plan_copy = pltpu.make_async_copy(plan_hbm, plan, sem.at[0])
    copies = [
        pltpu.make_async_copy(list_hbm, listing, sem.at[1]),
        pltpu.make_async_copy(v_hbm, vbuf, sem.at[2]),
    ]
    plan_copy.start()
    for copy in copies:
        copy.start()

    def p_copy(h):
        return pltpu.make_async_copy(p_hbm.at[h], pbuf.at[h], p_sem.at[h])

    def out_copy(h):
        return pltpu.make_async_copy(out_buf.at[:, lanes(h)], out_hbm.at[:, lanes(h)], out_sem.at[h])

    plan_copy.wait()

    @pl.loop(0, heads)
    def _(i):
        p_copy(plan[1, i]).start()

    def combine(members, count):
        for h in members:
            for qb in range(q_blocks):
                names = [jnp.maximum(listing[qb, k, m * heads + h], 0) for k in range(count)]
                values = jnp.concatenate([vbuf[b, :, lanes(h // PER_GROUP)] for b in names], axis=0)
                product = jnp.dot(
                    pbuf[h, parts[qb], :count * BLK], values, preferred_element_type=jnp.float32)
                out_buf[parts[qb], lanes(h)] = product.astype(out_buf.dtype)

    for copy in copies:
        copy.wait()
    steps = [kmax * i // 4 for i in range(1, 5)]

    @pl.loop(0, heads // together)
    def _(t):
        members = [plan[1, t * together + j] for j in range(together)]
        need = plan[0, m * heads + members[0]]
        for h in members:
            p_copy(h).wait()
        for below, high in zip([0] + steps, steps):
            @pl.when(jnp.logical_and(need > below, need <= high))
            def _():
                combine(members, high)

        for h in members:
            out_copy(h).start()

    @pl.loop(0, heads)
    def _(h):
        out_copy(h).wait()


def body(n_seq, n_mlp, query_rows, key_rows, value_rows, key_blocks):
    piece = key_rows.shape[0]
    rows = query_rows.shape[0]
    heads = H // n_mlp
    width = (KVH // n_mlp) * HD
    q_blocks, kmax = key_blocks.shape[1:]
    chips = n_seq // 2
    blocks = n_seq * n_mlp
    listing = jnp.transpose(key_blocks, (1, 2, 0))
    dma = pltpu.SemaphoreType.DMA
    whole = pl.BlockSpec(memory_space=pltpu.VMEM)
    anywhere = pl.BlockSpec(memory_space=pl.ANY)
    scalars = pl.BlockSpec(memory_space=pltpu.SMEM)
    room = 62 * 1024 * 1024
    values, probs, plan = pl.pallas_call(
        functools.partial(score_kernel, n_seq, n_mlp),
        out_shape=(
            jax.ShapeDtypeStruct((blocks, piece, width), jnp.bfloat16),
            jax.ShapeDtypeStruct((heads, rows, kmax * BLK), jnp.bfloat16),
            jax.ShapeDtypeStruct((8, H), jnp.int32),
        ),
        in_specs=[scalars, whole, anywhere, anywhere, anywhere],
        out_specs=(anywhere, anywhere, whole),
        scratch_shapes=[
            pltpu.VMEM((blocks, piece, width), jnp.bfloat16),
            pltpu.VMEM((rows, heads * HD), jnp.bfloat16),
            pltpu.VMEM((q_blocks, heads, kmax * BLK), jnp.float32),
            pltpu.VMEM((H, kmax * BLK), jnp.float32),
            pltpu.VMEM((heads, rows, kmax * BLK), jnp.bfloat16),
            dma((3,)),
            dma((heads,)),
            dma((2, n_mlp)),
            dma((2, n_mlp)),
            dma((2, n_mlp, chips)),
            dma((2, n_mlp, chips)),
            dma((2, n_mlp)),
            dma((2, n_mlp, chips)),
            dma((2, n_mlp, chips)),
        ],
        compiler_params=pltpu.CompilerParams(
            collective_id=0, has_side_effects=True, vmem_limit_bytes=room),
        name="gather_and_score",
    )(listing, listing, query_rows, key_rows, value_rows)
    return pl.pallas_call(
        combine_kernel,
        out_shape=jax.ShapeDtypeStruct((rows, heads * HD), jnp.bfloat16),
        in_specs=[anywhere] * 4,
        out_specs=anywhere,
        scratch_shapes=[
            pltpu.SMEM((q_blocks, kmax, H), jnp.int32),
            pltpu.SMEM((8, H), jnp.int32),
            pltpu.VMEM((heads, rows, kmax * BLK), jnp.bfloat16),
            pltpu.VMEM((blocks, piece, width), jnp.bfloat16),
            pltpu.VMEM((rows, heads * HD), jnp.bfloat16),
            dma((3,)),
            dma((heads,)),
            dma((heads,)),
        ],
        compiler_params=pltpu.CompilerParams(vmem_limit_bytes=room),
        name="combine_listed_values",
    )(listing, plan, probs, values)


def solution(mesh):
    placed = (
        P("seq", None),
        P(("seq", "mlp"), None),
        P(("seq", "mlp"), None),
        P(None, "seq", None),
    )
    return jax.shard_map(
        functools.partial(body, mesh.shape["seq"], mesh.shape["mlp"]),
        mesh=mesh, in_specs=placed, out_specs=P("seq", "mlp"), check_vma=False
    )
```

time: 52.1 us -> 36 us (0.69); the launches traced: 51.1 us -> 35.6 us
  Pallas kernels: 47.2 us -> 35.6 us
  local copies, waits for them, and re-layouts: 3.82 us -> 0 us
    pallas_call x1 -> x2, Pallas kernels: 47.2 us -> 35.6 us  [the longest x1 29.3 us: body(): pl.pallas_call(functools.partial(score_kernel, n_seq, n_mlp), out_shape=(...]
    unnamed x2 -> x0, local copies, waits for them, and re-layouts: 3.82 us -> none
where the time goes in v3:
time: 36 us; the launch traced here: 35.6 us
  Pallas kernels  35.6 us (99%)
    pallas_call x1, Pallas kernels, body(): pl.pallas_call(functools.partial(score_kernel, n_seq, n_mlp), out_shape=(...  29.3 us
    pallas_call x1, Pallas kernels, body(): pl.pallas_call(combine_kernel, out_shape=jax.ShapeDtypeStruct((rows, head...  6.23 us

profile of v3, /device:TPU:5, one launch (start us, length us, event | category | flops | bytes accessed | tf_op | source)
XLA Modules:
  0.0 35.6 jit_solution(12514421011183313484)
XLA Ops:
  0.0 29.3 %gather_and_score.1 = (bf16[32,64,256]{2,1,0:T(8,128)(2,1)}, bf16[16,256,1024]{2,1,0:T(8,128)(2,1)}, s32[8,64]{1,0:T(8,128)}) custom-call(s32[4,16,64]{2,1,0:T(8,128)} %bitcast.1, s32[4,16,64]{2,1,0:T(8,128)} %bitcast.2, bf16[256,8192]{1,0:T(8,128)(2,1)} %q_hbm.1, bf16[64,1024]{1,0:T(8,128)(2,1)} %k_hbm.1, bf16[64,1024]{1,0:T(8,128)(2,1)} %v_hbm.1), custom_call_target="tpu_custom_call" | custom-call | tf_op jit(solution)/shard_map/gather_and_score/pallas_call | solution.py:323
  29.3 6.2 %combine_listed_values.1 = bf16[256,2048]{1,0:T(8,128)(2,1)} custom-call(s32[4,16,64]{2,1,0:T(8,128)} %bitcast.3, s32[8,64]{1,0:T(8,128)} %get-tuple-element.8.plan_hbm, bf16[16,256,1024]{2,1,0:T(8,128)(2,1)} %get-tuple-element.9.p_hbm, bf16[32,64,256]{2,1,0:T(8,128)(2,1)} %get-tuple-element.10.v_hbm), custom_call_target="tpu_custom_call" | custom-call | tf_op jit(solution)/shard_map/combine_listed_values/pallas_call | solution.py:352

commit v4 on v3

--- a/solution.py
+++ b/solution.py
@@ -24,7 +24,7 @@
 
 
 def score_kernel(
-    n_seq, n_mlp, list_s, list_v, q_hbm, k_hbm, v_hbm, v_out, p_out, plan,
+    n_seq, n_mlp, list_s, list_v, q_hbm, k_hbm, v_hbm, v_out, p_out, k_out, kpos_out, plan,
     kbuf, qbuf, kpos, spaced, probs,
     local_sem, p_sem, z_send, z_recv, hop_send, hop_recv, own_sib_send, sib_send, sib_recv,
 ):
@@ -35,6 +35,7 @@
     width = kbuf.shape[2]
     q_blocks, kmax = list_v.shape[:2]
     heads = H // n_mlp
+    half = heads // 2
     together = 4 if kmax <= 16 else 1
     srcs = (k_hbm, v_hbm)
     bufs = (kbuf, v_out)
@@ -107,7 +108,7 @@
         return pltpu.make_async_copy(
             srcs[a].at[:, lanes(m, width)], bufs[a].at[s * n_mlp + m], local_sem.at[a])
 
-    q_copy = pltpu.make_async_copy(q_hbm.at[:, lanes(m, heads * HD)], qbuf, local_sem.at[2])
+    q_copy = pltpu.make_async_copy(q_hbm.at[:, lanes(2 * m, half * HD)], qbuf, local_sem.at[2])
     local_copy(0).start()
     local_copy(1).start()
 
@@ -149,35 +150,44 @@
     other = jnp.broadcast_to(used, (H, H))
     mine = jnp.sum(jnp.where(across == down, other, 0.0), axis=1, keepdims=True)
     ahead = jnp.logical_or(other > mine, jnp.logical_and(other == mine, across < down))
-    ahead = jnp.logical_and(ahead, across // heads == down // heads)
+    ahead = jnp.logical_and(ahead, across // half == down // half)
     rank = jnp.sum(jnp.where(ahead, 1.0, 0.0), axis=1, keepdims=True)
-    holds = jnp.logical_and(rank == across.astype(jnp.float32), down // heads == m)
-    order = jnp.sum(jnp.where(holds, (down - m * heads).astype(jnp.float32), 0.0), axis=0, keepdims=True)
+    local = (down - m * heads).astype(jnp.float32)
+
+    def order(which):
+        holds = jnp.logical_and(rank == across.astype(jnp.float32), down // half == 2 * m + which)
+        return jnp.sum(jnp.where(holds, local, 0.0), axis=0, keepdims=True)
+
     plan_row = lax.broadcasted_iota(jnp.int32, plan.shape, 0)
-    plan[...] = jnp.where(plan_row == 0, used, order).astype(jnp.int32)
+    rows = jnp.where(plan_row == 0, used, jnp.where(plan_row == 1, order(0), order(1)))
+    plan[...] = rows.astype(jnp.int32)
 
     spread = (lax.broadcasted_iota(jnp.int32, (kmax, kmax * BLK), 1) // BLK
               == lax.broadcasted_iota(jnp.int32, (kmax, kmax * BLK), 0)).astype(jnp.bfloat16)
-    inside = (lax.broadcasted_iota(jnp.int32, (heads, kmax * BLK), 1) % BLK).astype(jnp.float32)
+    inside = (lax.broadcasted_iota(jnp.int32, (half, kmax * BLK), 1) % BLK).astype(jnp.float32)
     for qb in range(q_blocks):
         named = list_v[qb].astype(jnp.float32).astype(jnp.bfloat16)
         spaced[...] = lax.dot_general(
             named, spread, (((0,), (0,)), ((), ())), preferred_element_type=jnp.float32)
-        block = spaced[pl.ds(pl.multiple_of(m * heads, heads), heads), :]
-        kpos[qb] = jnp.where(block < 0, FAR, block * BLK + inside)
+        for which, target in enumerate((kpos, kpos_out)):
+            block = spaced[pl.ds(pl.multiple_of((2 * m + which) * half, half), half), :]
+            target[qb] = jnp.where(block < 0, FAR, block * BLK + inside)
 
     @pl.loop(0, n_mlp)
     def _(i):
         pass_on(0, z_order(i))
 
     finish(0)
+    k_copy = pltpu.make_async_copy(kbuf.at[:, :, width // 2:], k_out, local_sem.at[3])
+    k_copy.start()
     q_copy.wait()
 
     factor = math.log2(math.e) / math.sqrt(HD)
     first = s * q_blocks * BLK
     parts = [slice(qb * BLK, (qb + 1) * BLK) for qb in range(q_blocks)]
     row_in_block = lax.broadcasted_iota(jnp.int32, (BLK, 1), 0)
-    steps = heads // together
+    steps = half // together
+    per = max(n_mlp // steps, 1)
 
     def p_copy(t):
         some = pl.ds(t * together, together)
@@ -210,10 +220,11 @@
             if j < together:
                 score(t * together + j, j)
         p_copy(t).start()
-        if steps == n_mlp:
-            pass_on(1, z_order(t))
-
-    if steps != n_mlp:
+        if per * steps == n_mlp:
+            for i in range(per):
+                pass_on(1, z_order(t * per + i))
+
+    if per * steps != n_mlp:
         @pl.loop(0, n_mlp)
         def _(i):
             pass_on(1, z_order(i))
@@ -223,6 +234,8 @@
     @pl.loop(0, steps)
     def _(t):
         p_copy(t).wait()
+
+    k_copy.wait()
 
     for a in range(2):
         @pl.loop(1, n_mlp)
@@ -244,21 +257,29 @@
                 sib_copy(a, z, src_p).wait_send()
 
 
-def combine_kernel(
-    list_hbm, plan_hbm, p_hbm, v_hbm, out_hbm, listing, plan, pbuf, vbuf, out_buf, sem, p_sem, out_sem,
+def finish_kernel(
+    list_hbm, plan_hbm, kpos, p_hbm, k_hbm, v_hbm, q_hbm, out_hbm,
+    listing, plan, pbuf, kbuf, vbuf, qbuf, out_buf, sem, p_sem, out_sem,
 ):
+    s = lax.axis_index("seq")
     m = lax.axis_index("mlp")
     q_blocks, kmax = listing.shape[:2]
-    heads = pbuf.shape[0]
+    half = pbuf.shape[0]
+    heads = 2 * half
+    base = half // PER_GROUP
     together = 4 if kmax <= 16 else 1
+    factor = math.log2(math.e) / math.sqrt(HD)
+    first = s * q_blocks * BLK
     parts = [slice(qb * BLK, (qb + 1) * BLK) for qb in range(q_blocks)]
-
-    plan_copy = pltpu.make_async_copy(plan_hbm, plan, sem.at[0])
+    row_in_block = lax.broadcasted_iota(jnp.int32, (BLK, 1), 0)
+
     copies = [
+        pltpu.make_async_copy(plan_hbm, plan, sem.at[0]),
         pltpu.make_async_copy(list_hbm, listing, sem.at[1]),
-        pltpu.make_async_copy(v_hbm, vbuf, sem.at[2]),
+        pltpu.make_async_copy(q_hbm.at[:, lanes(2 * m + 1, half * HD)], qbuf, sem.at[2]),
+        pltpu.make_async_copy(k_hbm, kbuf, sem.at[3]),
+        pltpu.make_async_copy(v_hbm, vbuf, sem.at[4]),
     ]
-    plan_copy.start()
     for copy in copies:
         copy.start()
 
@@ -268,13 +289,48 @@
     def out_copy(h):
         return pltpu.make_async_copy(out_buf.at[:, lanes(h)], out_hbm.at[:, lanes(h)], out_sem.at[h])
 
-    plan_copy.wait()
-
-    @pl.loop(0, heads)
-    def _(i):
-        p_copy(plan[1, i]).start()
-
-    def combine(members, count):
+    @pl.loop(0, half)
+    def _(h):
+        p_copy(h).start()
+
+    def attend(members, count):
+        places = [
+            [[jnp.maximum(listing[qb, k, m * heads + h], 0) for k in range(count)]
+             for qb in range(q_blocks)] for h in members]
+        scores, weights, totals = {}, {}, {}
+
+        def gathered(buf, j, qb):
+            group = lanes(members[j] // PER_GROUP - base) if buf is kbuf else lanes(members[j] // PER_GROUP)
+            return jnp.concatenate([buf[b, :, group] for b in places[j][qb]], axis=0)
+
+        def score(j):
+            for qb in range(q_blocks):
+                scores[j, qb] = lax.dot_general(
+                    qbuf[parts[qb], lanes(members[j] - half)], gathered(kbuf, j, qb), (((1,), (1,)), ((), ())),
+                    preferred_element_type=jnp.float32)
+
+        def weigh(j):
+            for qb in range(q_blocks):
+                row = (row_in_block + (first + qb * BLK)).astype(jnp.float32)
+                position = kpos[qb, pl.ds(members[j] - half, 1), :count * BLK]
+                masked = jnp.where(position <= row, scores.pop((j, qb)), MASKED)
+                top = jnp.max(masked, axis=1, keepdims=True)
+                raised = jnp.exp2((masked - top) * factor)
+                totals[j, qb] = jnp.sum(raised, axis=1, keepdims=True)
+                weights[j, qb] = raised.astype(jnp.bfloat16)
+
+        def combine(j):
+            for qb in range(q_blocks):
+                product = jnp.dot(
+                    weights.pop((j, qb)), gathered(vbuf, j, qb), preferred_element_type=jnp.float32)
+                out_buf[parts[qb], lanes(members[j])] = (product / totals.pop((j, qb))).astype(out_buf.dtype)
+
+        for step in range(len(members) + 2):
+            for stage, lag in ((combine, 2), (weigh, 1), (score, 0)):
+                if 0 <= step - lag < len(members):
+                    stage(step - lag)
+
+    def apply(members, count):
         for h in members:
             for qb in range(q_blocks):
                 names = [jnp.maximum(listing[qb, k, m * heads + h], 0) for k in range(count)]
@@ -287,19 +343,26 @@
         copy.wait()
     steps = [kmax * i // 4 for i in range(1, 5)]
 
-    @pl.loop(0, heads // together)
-    def _(t):
-        members = [plan[1, t * together + j] for j in range(together)]
-        need = plan[0, m * heads + members[0]]
-        for h in members:
-            p_copy(h).wait()
-        for below, high in zip([0] + steps, steps):
-            @pl.when(jnp.logical_and(need > below, need <= high))
-            def _():
-                combine(members, high)
-
-        for h in members:
-            out_copy(h).start()
+    def run(act, row):
+        @pl.loop(0, half // together)
+        def _(t):
+            members = [plan[row, t * together + j] for j in range(together)]
+            need = plan[0, m * heads + members[0]]
+            for below, high in zip([0] + steps, steps):
+                @pl.when(jnp.logical_and(need > below, need <= high))
+                def _():
+                    act(members, high)
+
+            for h in members:
+                out_copy(h).start()
+
+    run(attend, 2)
+
+    @pl.loop(0, half)
+    def _(h):
+        p_copy(h).wait()
+
+    run(apply, 1)
 
     @pl.loop(0, heads)
     def _(h):
@@ -310,6 +373,7 @@
     piece = key_rows.shape[0]
     rows = query_rows.shape[0]
     heads = H // n_mlp
+    half = heads // 2
     width = (KVH // n_mlp) * HD
     q_blocks, kmax = key_blocks.shape[1:]
     chips = n_seq // 2
@@ -320,23 +384,25 @@
     anywhere = pl.BlockSpec(memory_space=pl.ANY)
     scalars = pl.BlockSpec(memory_space=pltpu.SMEM)
     room = 62 * 1024 * 1024
-    values, probs, plan = pl.pallas_call(
+    values, probs, keys, kpos, plan = pl.pallas_call(
         functools.partial(score_kernel, n_seq, n_mlp),
         out_shape=(
             jax.ShapeDtypeStruct((blocks, piece, width), jnp.bfloat16),
-            jax.ShapeDtypeStruct((heads, rows, kmax * BLK), jnp.bfloat16),
+            jax.ShapeDtypeStruct((half, rows, kmax * BLK), jnp.bfloat16),
+            jax.ShapeDtypeStruct((blocks, piece, width // 2), jnp.bfloat16),
+            jax.ShapeDtypeStruct((q_blocks, half, kmax * BLK), jnp.float32),
             jax.ShapeDtypeStruct((8, H), jnp.int32),
         ),
         in_specs=[scalars, whole, anywhere, anywhere, anywhere],
-        out_specs=(anywhere, anywhere, whole),
+        out_specs=(anywhere, anywhere, anywhere, whole, whole),
         scratch_shapes=[
             pltpu.VMEM((blocks, piece, width), jnp.bfloat16),
-            pltpu.VMEM((rows, heads * HD), jnp.bfloat16),
-            pltpu.VMEM((q_blocks, heads, kmax * BLK), jnp.float32),
+            pltpu.VMEM((rows, half * HD), jnp.bfloat16),
+            pltpu.VMEM((q_blocks, half, kmax * BLK), jnp.float32),
             pltpu.VMEM((H, kmax * BLK), jnp.float32),
-            pltpu.VMEM((heads, rows, kmax * BLK), jnp.bfloat16),
-            dma((3,)),
-            dma((heads,)),
+            pltpu.VMEM((half, rows, kmax * BLK), jnp.bfloat16),
+            dma((4,)),
+            dma((half,)),
             dma((2, n_mlp)),
             dma((2, n_mlp)),
             dma((2, n_mlp, chips)),
@@ -350,23 +416,25 @@
         name="gather_and_score",
     )(listing, listing, query_rows, key_rows, value_rows)
     return pl.pallas_call(
-        combine_kernel,
+        finish_kernel,
         out_shape=jax.ShapeDtypeStruct((rows, heads * HD), jnp.bfloat16),
-        in_specs=[anywhere] * 4,
+        in_specs=[anywhere, anywhere, whole, anywhere, anywhere, anywhere, anywhere],
         out_specs=anywhere,
         scratch_shapes=[
             pltpu.SMEM((q_blocks, kmax, H), jnp.int32),
             pltpu.SMEM((8, H), jnp.int32),
-            pltpu.VMEM((heads, rows, kmax * BLK), jnp.bfloat16),
+            pltpu.VMEM((half, rows, kmax * BLK), jnp.bfloat16),
+            pltpu.VMEM((blocks, piece, width // 2), jnp.bfloat16),
             pltpu.VMEM((blocks, piece, width), jnp.bfloat16),
+            pltpu.VMEM((rows, half * HD), jnp.bfloat16),
             pltpu.VMEM((rows, heads * HD), jnp.bfloat16),
-            dma((3,)),
-            dma((heads,)),
+            dma((5,)),
+            dma((half,)),
             dma((heads,)),
         ],
         compiler_params=pltpu.CompilerParams(vmem_limit_bytes=room),
-        name="combine_listed_values",
-    )(listing, plan, probs, values)
+        name="attend_and_combine",
+    )(listing, plan, kpos, probs, keys, values, query_rows)
 
 
 def solution(mesh):

time: 36 us -> 35 us (0.972)
  Pallas kernels: 35.6 us -> 34.7 us
    pallas_call x1, Pallas kernels: 29.3 us -> 25.3 us  [body(): pl.pallas_call(functools.partial(score_kernel, n_seq, n_mlp), out_shape=(...]
    pallas_call x1, Pallas kernels: 6.23 us -> 9.42 us  [body(): pl.pallas_call(finish_kernel, out_shape=jax.ShapeDtypeStruct((rows, heads...]
where the time goes in v4:
time: 35 us; the launch traced here: 34.7 us
  Pallas kernels  34.7 us (99%)
    pallas_call x1, Pallas kernels, body(): pl.pallas_call(functools.partial(score_kernel, n_seq, n_mlp), out_shape=(...  25.3 us
    pallas_call x1, Pallas kernels, body(): pl.pallas_call(finish_kernel, out_shape=jax.ShapeDtypeStruct((rows, heads...  9.42 us

profile of v4, /device:TPU:5, one launch (start us, length us, event | category | flops | bytes accessed | tf_op | source)
XLA Modules:
  0.0 34.7 jit_solution(11095948846990796680)
XLA Ops:
  0.0 25.3 %gather_and_score.1 = (bf16[32,64,256]{2,1,0:T(8,128)(2,1)}, bf16[8,256,1024]{2,1,0:T(8,128)(2,1)}, bf16[32,64,128]{2,1,0:T(8,128)(2,1)}, f32[4,8,1024]{2,1,0:T(8,128)}, s32[8,64]{1,0:T(8,128)}) custom-call(s32[4,16,64]{2,1,0:T(8,128)} %bitcast.1, s32[4,16,64]{2,1,0:T(8,128)} %bitcast.2, bf16[256,8192]{1,0:T(8,128)(2,1)} %q_hbm.3, bf16[64,1024]{1,0:T(8,128)(2,1)} %k_hbm.1, ...), custom_call_target="tpu_custom_call" | custom-call | tf_op jit(solution)/shard_map/gather_and_score/pallas_call | solution.py:387
  25.3 9.4 %attend_and_combine.1 = bf16[256,2048]{1,0:T(8,128)(2,1)} custom-call(s32[4,16,64]{2,1,0:T(8,128)} %bitcast.3, s32[8,64]{1,0:T(8,128)} %get-tuple-element.10.plan_hbm, f32[4,8,1024]{2,1,0:T(8,128)} %get-tuple-element.11.kpos, bf16[8,256,1024]{2,1,0:T(8,128)(2,1)} %get-tuple-element.12.p_hbm, bf16[32,64,128]{2,1,0:T(8,128)(2,1)} %get-tuple-element.13.k_hbm, ...), custom_call_target="tpu_custom_call" | custom-call | tf_op jit(solution)/shard_map/attend_and_combine/pallas_call | solution.py:418
